TPU v7x, 256 devices: a whole 4x4x8 slice. The times are simulated.
256 devices in a mesh: slab: 64 (over z, y, core), tile: 4 (over x).
Axes of the slice: x: 4, y: 4, z: 8, core: 2. Of those that a mesh axis runs over, the one named last changes fastest.
Arguments:
- snapshots: bfloat16 [8192, 128, 256], P(('slab', 'tile')), may hold values from -1210 to 1210
- routes: int32 [8192, 1], P(('slab', 'tile')), may hold values from 0 to 3; in each aligned block of 32 rows (0 to 31, 32 to 63, ...) at most 10 rows name the same one
- sketch_matrix: bfloat16 [256, 128], replicated, may hold values from -0.375 to 0.375
Outputs:
- basis_rows: bfloat16 [10240, 128, 128], P(('slab', 'tile'))
- triangle: float32 [128, 128], replicated
Inputs may be any that keep to these rules, and one draw needn't show every extreme that they name: `routes`: among the 32 blocks of one device no owner value appears more than 10 times; a block with value o goes to tile o of its own slab.
All inputs are finite; a program needn't handle non-finite values.
Results may differ from a plain program's by a relative error of at most 0.0065.
Values may be sent and summed in bfloat16 or wider, within the bound.
A program may use at most 64 MiB of HBM per device.

v0:
```python
import math
import jax
import jax.numpy as jnp
from jax import lax
from jax.sharding import PartitionSpec as P

SEND = 10


def slot_selector(routes, tiles, slots):
    destination = routes[:, 0]
    owners = jnp.arange(tiles, dtype=jnp.int32)
    owner_hit = (destination[None, :] == owners[:, None]).astype(jnp.int32)
    earlier = jnp.cumsum(owner_hit, axis=1) - owner_hit
    slot_ids = jnp.arange(slots, dtype=jnp.int32)
    chosen = owner_hit[:, None, :] * (earlier[:, None, :] == slot_ids[None, :, None]).astype(
        jnp.int32
    )
    return chosen.reshape(tiles * slots, routes.shape[0]).astype(jnp.bfloat16)


def place_blocks(selector, block_data):
    block_count, cell_rows, width = block_data.shape
    flattened = jnp.dot(
        selector,
        block_data.reshape(block_count, cell_rows * width),
        preferred_element_type=jnp.float32,
    )
    return flattened.astype(jnp.bfloat16).reshape(selector.shape[0], cell_rows, width)


def global_factor(partial_gram):
    gram_matrix = lax.psum(partial_gram, ("slab", "tile"))
    return jnp.linalg.cholesky(gram_matrix)


def local(snapshots, routes, sketch_matrix):
    n_tile = lax.axis_size("tile")
    n_slab = lax.axis_size("slab")
    block_count, cell_rows, snap_width = snapshots.shape
    sketch_width = sketch_matrix.shape[1]
    cell_root = math.sqrt(block_count * cell_rows * n_slab * n_tile)
    selector = slot_selector(routes, n_tile, SEND)
    outgoing = place_blocks(selector, snapshots).reshape(n_tile, SEND, cell_rows, snap_width)
    product = jnp.einsum(
        "tjrc,cd->tjrd",
        lax.all_to_all(outgoing, "tile", split_axis=0, concat_axis=0, tiled=True),
        sketch_matrix,
        preferred_element_type=jnp.float32,
    )
    sketch = product.astype(jnp.bfloat16)
    sketch_rows = sketch.reshape(-1, sketch_width)
    partial_gram = lax.dot_general(
        sketch_rows, sketch_rows, (((0,), (0,)), ((), ())), preferred_element_type=jnp.float32
    )
    lower_factor = global_factor(partial_gram)
    identity = jnp.eye(sketch_width, dtype=jnp.float32)
    inverse_factor = jax.scipy.linalg.solve_triangular(lower_factor, identity, lower=True)
    wide_rows = sketch_rows.astype(jnp.float32)
    scaled = (
        jnp.dot(wide_rows, inverse_factor.T, precision=lax.Precision.HIGHEST) * cell_root
    ).astype(jnp.bfloat16)
    basis_rows = scaled.reshape(n_tile * SEND, cell_rows, sketch_width)
    return (basis_rows, lower_factor.T / cell_root)


def solution(mesh):
    return jax.shard_map(
        local,
        mesh=mesh,
        in_specs=(P(("slab", "tile"), None, None), P(("slab", "tile"), None), P()),
        out_specs=(P(("slab", "tile"), None, None), P()),
        check_vma=False,
    )
```

profile of v0, /device:TPU:1, one launch (start us, length us, event | category | flops | bytes accessed | tf_op | source)
XLA Modules:
  0.0 325.9 jit_solution(3418719268438397038)
XLA Ops:
  7.2 0.0 copy-start
  7.2 0.0 all-reduce.2.cloned.1.call-start
  7.2 0.7 fusion.5
  7.9 0.2 reduce_window_sum.11
  8.1 0.7 fusion.6
  8.8 2.8 copy.17
  11.6 0.8 convolution_convert_fusion
  12.4 0.6 copy.18
  13.0 35.5 %all_to_all.5 = bf16[4,10,128,256]{3,2,1,0:T(8,128)(2,1)S(1)} all-to-all(bf16[4,10,128,256]{3,2,1,0:T(8,128)(2,1)S(1)} %bitcast.35), channel_id=1, replica_groups=mesh['slab'=64,'tile'=4] {'tile'}, dimensions={0} | all-to-all | bytes 5242880 | tf_op jit(solution)/shard_map/all_to_all | solution.py:47
  48.6 0.0 copy-done
  48.6 0.8 convolution_convert_fusion.1
  49.4 1.2 convolution_bitcast_fusion
  50.6 0.0 all-reduce.2.cloned.1.call-update
  50.6 240.6 %all-reduce.2.cloned.1.call-done = f32[128,128]{0,1:T(8,128)} async-done(((f32[128,128]{0,1:T(8,128)}), f32[128,128]{0,1:T(8,128)}) %all-reduce.2.cloned.1.call-update) | async-done | bytes 65552 | tf_op jit(solution)/shard_map/psum | solution.py:33
  291.2 0.9 copy.11
  292.1 0.9 fusion.4
  293.0 11.7 %cholesky.17 = f32[128,128]{1,0:T(8,128)S(1)} custom-call(f32[128,128]{1,0:T(8,128)S(1)} %fusion.4), custom_call_target="Cholesky" | custom-call | tf_op jit(solution)/shard_map/jit(cholesky)/cholesky | solution.py:34
  304.7 0.6 compare_reduce_fusion
  305.4 0.7 multiply_bitcast_fusion
  306.0 0.7 copy.12
  306.8 9.8 %custom-call.7 = f32[1,128,128]{1,2,0:T(8,128)S(1)} custom-call(f32[1,128,128]{2,1,0:T(8,128)S(1)} %get-tuple-element.7), custom_call_target="InvertDiagBlocksLowerTriangular" | custom-call | tf_op jit(solution)/shard_map/jit(_solve_triangular)/triangular_solve | solution.py:58
  316.6 0.2 fusion.2
  316.8 2.3 fusion
  (3 shorter events, 0.1 us)
Async XLA Ops:
  7.2 41.4 %copy-start = (bf16[256,128]{1,0:T(8,128)(2,1)S(1)}, bf16[256,128]{1,0:T(8,128)(2,1)}, u32[]{:S(2)}) copy-start(bf16[256,128]{1,0:T(8,128)(2,1)} %param.5) | copy-start | bytes 196612
  7.2 284.0 %all-reduce.2.cloned.1.call-start = ((), (), s32[]{:S(2)}) async-start(), calls=%async_computation.1 | async-start | bytes 131072 | tf_op jit(solution)/shard_map/psum | solution.py:33
Sparse Core Ops, SparseCore 0:
  50.7 240.4 all-reduce.1
where the time goes:
time: 326 us
  waiting for transfers between devices  241 us (74%)
  blocking collectives  35.5 us (11%)
  other arithmetic  25.2 us (8%)
  between operations  14.1 us (4%)
  matrix products  5.37 us (2%)
  local copies, waits for them, and re-layouts  5.09 us (2%)
    psum x1, waiting for transfers between devices, global_factor(): gram_matrix = lax.psum(partial_gram, ('slab', 'tile'))  241 us
    all_to_all x1, blocking collectives, local(): lax.all_to_all(outgoing, 'tile', split_axis=0, concat_axis=0, tiled=True)  35.5 us
    another operation x3, other arithmetic, global_factor(): return jnp.linalg.cholesky(gram_matrix)  12.4 us
    another operation x1, other arithmetic, local(): jax.scipy.linalg.solve_triangular(lower_factor, identity, lower=True)  9.81 us
  transfers between devices with their start and end apart: 1, of which 1 were waited for; matrix products, arithmetic and copies ran while one was open for 0% of the time, Pallas kernels for 0%

commit v1 on v0

--- a/solution.py
+++ b/solution.py
@@ -30,7 +30,8 @@
 
 
 def global_factor(partial_gram):
-    gram_matrix = lax.psum(partial_gram, ("slab", "tile"))
+    perform_orders_by_axis = lambda sample: lax.all_gather(sample, ("slab", "tile")).sum(axis=0)
+    gram_matrix = perform_orders_by_axis(partial_gram)
     return jnp.linalg.cholesky(gram_matrix)
 
 

time: 326 us -> 218 us (0.67)
  waiting for transfers between devices: 241 us -> 128 us
  other arithmetic: 25.2 us -> 31 us
    psum x1 -> x0, waiting for transfers between devices: 241 us -> none  [global_factor(): gram_matrix = lax.psum(partial_gram, ('slab', 'tile'))]
    all_gather x0 -> x1, waiting for transfers between devices: none -> 128 us  [global_factor(): lax.all_gather(sample, ('slab', 'tile')).sum(axis=0)]
    reduce_sum x0 -> x1, other arithmetic: none -> 6.59 us  [global_factor(): lax.all_gather(sample, ('slab', 'tile')).sum(axis=0)]
where the time goes in v1:
time: 218 us
  waiting for transfers between devices  128 us (59%)
  blocking collectives  35.5 us (16%)
  other arithmetic  31 us (14%)
  between operations  14.1 us (6%)
  matrix products  5.36 us (2%)
  local copies, waits for them, and re-layouts  4.25 us (2%)
    all_gather x1, waiting for transfers between devices, global_factor(): lax.all_gather(sample, ('slab', 'tile')).sum(axis=0)  128 us
    all_to_all x1, blocking collectives, local(): lax.all_to_all(outgoing, 'tile', split_axis=0, concat_axis=0, tiled=True)  35.5 us
    another operation x3, other arithmetic, global_factor(): return jnp.linalg.cholesky(gram_matrix)  12.4 us
    another operation x1, other arithmetic, local(): jax.scipy.linalg.solve_triangular(lower_factor, identity, lower=True)  9.81 us
    reduce_sum x1, other arithmetic, global_factor(): lax.all_gather(sample, ('slab', 'tile')).sum(axis=0)  6.59 us
  transfers between devices with their start and end apart: 1, of which 1 were waited for; matrix products, arithmetic and copies ran while one was open for 0% of the time, Pallas kernels for 0%

profile of v1, /device:TPU:1, one launch (start us, length us, event | category | flops | bytes accessed | tf_op | source)
XLA Modules:
  0.0 218.1 jit_solution(12798227292656291407)
XLA Ops:
  7.2 0.0 copy-start
  7.2 0.0 all-gather.3.cloned.1.call-start
  7.2 0.7 fusion.5
  7.9 0.2 reduce_window_sum.11
  8.1 0.7 fusion.6
  8.8 2.8 %copy.17 = bf16[4,8,128,256]{3,1,2,0:T(8,128)(2,1)S(1)} copy(bf16[4,8,128,256]{3,2,1,0:T(8,128)(2,1)} %bitcast.41) | data formatting | bytes 4194304
  11.6 0.8 convolution_convert_fusion
  12.4 0.6 copy.18
  13.0 35.5 %all_to_all.5 = bf16[4,10,128,256]{3,2,1,0:T(8,128)(2,1)S(1)} all-to-all(bf16[4,10,128,256]{3,2,1,0:T(8,128)(2,1)S(1)} %bitcast.39), channel_id=1, replica_groups=mesh['slab'=64,'tile'=4] {'tile'}, dimensions={0} | all-to-all | bytes 5242880 | tf_op jit(solution)/shard_map/all_to_all | solution.py:48
  48.6 0.0 copy-done
  48.6 0.8 convolution_convert_fusion.1
  49.4 1.2 convolution_bitcast_fusion
  50.6 0.0 all-gather.3.cloned.1.call-update
  50.6 127.9 %all-gather.3.cloned.1.call-done = f32[32768,128]{1,0:T(8,128)} async-done(((f32[128,128]{1,0:T(8,128)}), f32[32768,128]{1,0:T(8,128)}) %all-gather.3.cloned.1.call-update) | async-done | bytes 16777232 | tf_op jit(solution)/shard_map/all_gather | solution.py:33
  178.5 6.6 %reduce_sum.9 = f32[128,128]{1,0:T(8,128)S(1)} reduce(f32[256,128,128]{2,1,0:T(8,128)} %bitcast.37, f32[]{:T(128)} %constant.48.clone.1), dimensions={0}, to_apply=%region_1.2 | reduce | flops 4177920 | bytes 16842756 | tf_op jit(solution)/shard_map/reduce_sum | solution.py:33
  185.1 0.1 copy.12
  185.2 11.7 %cholesky.17 = f32[128,128]{1,0:T(8,128)S(1)} custom-call(f32[128,128]{1,0:T(8,128)S(1)} %fusion.4), custom_call_target="Cholesky" | custom-call | tf_op jit(solution)/shard_map/jit(cholesky)/cholesky | solution.py:35
  196.9 0.6 compare_reduce_fusion
  197.6 0.7 multiply_bitcast_fusion
  198.2 0.7 copy.13
  199.0 9.8 %custom-call.7 = f32[1,128,128]{1,2,0:T(8,128)S(1)} custom-call(f32[1,128,128]{2,1,0:T(8,128)S(1)} %get-tuple-element.9), custom_call_target="InvertDiagBlocksLowerTriangular" | custom-call | tf_op jit(solution)/shard_map/jit(_solve_triangular)/triangular_solve | solution.py:59
  208.8 0.2 fusion.2
  209.0 2.3 %fusion = bf16[5120,128]{1,0:T(8,128)(2,1)} fusion(bf16[5120,128]{1,0:T(8,128)(2,1)S(1)} %bitcast.36, f32[128,128]{1,0:T(8,128)S(1)} %fusion.2), kind=kOutput, calls=%fused_computation.2 | convolution fusion | flops 1007943680 | bytes 2686976 | tf_op jit(solution)/shard_map/dot_general | solution.py:62
  (4 shorter events, 0.1 us)
Async XLA Ops:
  7.2 41.4 %copy-start = (bf16[256,128]{1,0:T(8,128)(2,1)S(1)}, bf16[256,128]{1,0:T(8,128)(2,1)}, u32[]{:S(2)}) copy-start(bf16[256,128]{1,0:T(8,128)(2,1)} %param.5) | copy-start | bytes 196612
  7.2 171.3 %all-gather.3.cloned.1.call-start = ((), (), s32[]{:S(2)}) async-start(), calls=%async_computation.1 | async-start | bytes 16842752 | tf_op jit(solution)/shard_map/all_gather | solution.py:33
Sparse Core Ops, SparseCore 0:
  50.7 127.6 all-gather.2
